TPU v7x, 256 devices: a whole 4x4x8 slice. The times are simulated.
256 devices in a mesh: dp: 16 (over z_hi, x, core), slot: 4 (over y), hid: 4 (over z_lo).
Axes of the slice: x: 4, y: 4, z: 8 (z_hi: 2, z_lo: 4; z = z_hi * 4 + z_lo), core: 2. Of those that a mesh axis runs over, the one named last changes fastest.
Arguments:
- master_weights: float32 [8, 3, 768, 2048], P('slot', None, 'hid', 'dp'), may hold values from -0.125 to 0.125
- first_moment: float32 [8, 3, 768, 2048], P('slot', None, 'hid', 'dp'), may hold values from -6 to 6
- second_moment: float32 [8, 3, 768, 2048], P('slot', None, 'hid', 'dp'), may hold values from 1 to 100
- tokens_one: bfloat16 [16384, 2048], P('dp'), may hold values from -6 to 6
- grad_out: bfloat16 [16384, 2048], P('dp'), may hold values from -6 to 6
- route_one: int32 [16384, 2], P('dp'), may hold values from 0 to 7, all different within a row
- prob_one: float32 [16384, 2], P('dp'), may hold values from 0.05 to 0.6
- tokens_two: bfloat16 [16384, 2048], P('dp'), may hold values from -6 to 6
- route_two: int32 [16384, 2], P('dp'), may hold values from 0 to 7, all different within a row
- prob_two: float32 [16384, 2], P('dp'), may hold values from 0.05 to 0.6
- old_order: int32 [8], replicated, may hold values from 0 to 7, each once
- new_order: int32 [8], replicated, may hold values from 0 to 7, each once
Outputs:
- moved_master: float32 [8, 3, 768, 2048], P('slot', None, 'hid', 'dp')
- moved_first: float32 [8, 3, 768, 2048], P('slot', None, 'hid', 'dp')
- moved_second: float32 [8, 3, 768, 2048], P('slot', None, 'hid', 'dp')
- next_output: bfloat16 [16384, 2048], P('dp', ('slot', 'hid'))
Inputs may be any that keep to these rules, and one draw needn't show every extreme that they name: `old_order`: lists each of the 8 experts once. `new_order`: lists each of the 8 experts once. `route_one`: each row names 2 different experts. `route_two`: each row names 2 different experts.
All inputs are finite; a program needn't handle non-finite values.
Results may differ from a plain program's by a relative error of at most 0.017.
Values may be sent and summed in bfloat16 or wider, within the bound.
No kernel may reach another device: no remote copies, remote signals or barrier semaphores. Data moves between devices by JAX's collectives and lax.ppermute only.
A program may use at most 128 MiB of HBM per device.

v0:
```python
import jax
import jax.numpy as jnp
from jax import lax
from jax.sharding import Mesh
from jax.sharding import PartitionSpec as P

DP = ("dp_0", "dp_1", "dp_2")
learn_rate = 0.001
beta_one = 0.9
beta_two = 0.95
epsilon = 1e-08
decay_rate = 0.1


def in_blocks(x, dim, size):
    before, after = (x.shape[:dim], x.shape[dim + 1 :])
    return jnp.moveaxis(x.reshape(*before, size, -1, *after), dim, 0)


def summed_rows(x, chips, core, dim):
    sizes = (lax.axis_size(chips), lax.axis_size(core))
    pieces = in_blocks(x, dim, sizes[0] * sizes[1])
    inside = pieces.shape[1:]
    pieces = pieces.reshape(*sizes, *inside).swapaxes(0, 1).reshape(-1, *inside)
    pieces = lax.psum_scatter(pieces, core, scatter_dimension=0, tiled=True)
    return lax.psum_scatter(pieces, chips, scatter_dimension=0, tiled=True)[0]


def scatter_axes(x, axes, dim):
    if not axes:
        return x
    nearer = lax.psum_scatter(x, axes[0], scatter_dimension=dim, tiled=True)
    return scatter_axes(nearer, axes[1:], dim)


def rows_by(left, right):
    return lax.dot_general(
        left, right, (((1,), (1,)), ((), ())), preferred_element_type=jnp.float32
    )


def cols_by(left, right):
    return lax.dot_general(
        left, right, (((0,), (0,)), ((), ())), preferred_element_type=jnp.float32
    )


def expert_parts(tokens, grad_out, scaling, weights):
    gate_proj = rows_by(tokens, weights[0])
    up_proj = rows_by(tokens, weights[1])
    logistic = jax.nn.sigmoid(gate_proj)
    swish_gate = gate_proj * logistic
    activated = (swish_gate * up_proj).astype(jnp.bfloat16)
    scaled_grad = (scaling[:, None] * grad_out.astype(jnp.float32)).astype(jnp.bfloat16)
    d_activated = rows_by(scaled_grad, weights[2])
    d_gate = (d_activated * up_proj * logistic * (1.0 + gate_proj * (1.0 - logistic))).astype(
        jnp.bfloat16
    )
    d_up = (d_activated * swish_gate).astype(jnp.bfloat16)
    return (d_gate, d_up, activated, scaled_grad)


def expert_out(tokens, scaling, weights):
    gate_proj = rows_by(tokens, weights[0])
    up_proj = rows_by(tokens, weights[1])
    mixed = (scaling[:, None] * gate_proj * jax.nn.sigmoid(gate_proj) * up_proj).astype(
        jnp.bfloat16
    )
    return jnp.dot(mixed, weights[2], preferred_element_type=jnp.float32)


def adamw_update(master, moment_a, moment_b, grad_sum):
    new_a = beta_one * moment_a + (1.0 - beta_one) * grad_sum
    new_b = beta_two * moment_b + (1.0 - beta_two) * grad_sum * grad_sum
    fixed_a = new_a / (1.0 - beta_one**10)
    fixed_b = new_b / (1.0 - beta_two**10)
    new_master = master - learn_rate * (
        fixed_a / (jnp.sqrt(fixed_b) + epsilon) + decay_rate * master
    )
    return (new_master, new_a, new_b)


def coefficients(routes, probs, expert_ids):
    matches = routes[:, :, None] == expert_ids[None, None, :]
    return jnp.sum(jnp.where(matches, probs[:, :, None], 0.0), axis=1)


def per_device(
    master_weights,
    first_moment,
    second_moment,
    tokens_one,
    grad_out,
    route_one,
    prob_one,
    tokens_two,
    route_two,
    prob_two,
    old_order,
    new_order,
):
    local_count = master_weights.shape[0]
    slot_index = lax.axis_index("slot")
    slot_count = lax.axis_size("slot")
    offset = slot_index * local_count
    held_ids = lax.dynamic_slice_in_dim(old_order, offset, local_count)
    shard_weights = master_weights.astype(jnp.bfloat16)
    full_weights = lax.all_gather(shard_weights, DP, axis=3, tiled=True)
    scaling_one = coefficients(route_one, prob_one, held_ids)
    parts = [
        expert_parts(tokens_one, grad_out, scaling_one[:, expert], full_weights[expert])
        for expert in range(local_count)
    ]
    gradients = jnp.stack(
        [
            jnp.stack(
                [
                    cols_by(part[0], tokens_one),
                    cols_by(part[1], tokens_one),
                    cols_by(part[2], part[3]),
                ]
            )
            for part in parts
        ]
    )
    owned_grads = summed_rows(gradients.astype(jnp.bfloat16), ("dp_0", "dp_1"), "dp_2", 3).astype(
        jnp.float32
    )
    new_master, new_a, new_b = adamw_update(
        master_weights, first_moment, second_moment, owned_grads
    )
    positions = jnp.arange(old_order.shape[0], dtype=jnp.int32)
    source = jnp.sum(
        jnp.where(old_order[None, :] == new_order[:, None], positions[None, :], 0), axis=1
    )
    owner_slot = source // local_count
    within = source % local_count
    my_owners = lax.dynamic_slice_in_dim(owner_slot, offset, local_count)
    pick_rows = my_owners * local_count + jnp.arange(local_count, dtype=jnp.int32)

    def outgoing(state_block):
        picked = jnp.take(state_block, within, axis=0)
        return picked.reshape((slot_count, local_count) + state_block.shape[1:])

    arrived = (
        lax.all_to_all(outgoing(new_master), "slot", split_axis=0, concat_axis=0, tiled=True),
        lax.all_to_all(outgoing(new_a), "slot", split_axis=0, concat_axis=0, tiled=True),
        lax.all_to_all(outgoing(new_b), "slot", split_axis=0, concat_axis=0, tiled=True),
    )
    moved_states = tuple(
        (
            jnp.take(
                state_block.reshape((slot_count * local_count,) + state_block.shape[2:]),
                pick_rows,
                axis=0,
            )
            for state_block in arrived
        )
    )
    moved_master, moved_first, moved_second = moved_states
    next_shard = new_master.astype(jnp.bfloat16)
    next_full = lax.all_gather(next_shard, DP, axis=3, tiled=True)
    scaling_two = coefficients(route_two, prob_two, held_ids)
    partial_value = expert_out(tokens_two, scaling_two[:, 0], next_full[0])
    expert = 1
    partial_value = partial_value + expert_out(
        tokens_two, scaling_two[:, expert], next_full[expert]
    )
    mixed_out = scatter_axes(partial_value, ("slot", "hid"), 1).astype(jnp.bfloat16)
    return (moved_master, moved_first, moved_second, mixed_out)


def solution(mesh):
    split = Mesh(
        mesh.devices.reshape(2, 4, 2, mesh.shape["slot"], mesh.shape["hid"]),
        ("dp_0", "dp_1", "dp_2", "slot", "hid"),
    )
    in_specs = (
        P("slot", None, "hid", DP),
        P("slot", None, "hid", DP),
        P("slot", None, "hid", DP),
        P(DP, None),
        P(DP, None),
        P(DP, None),
        P(DP, None),
        P(DP, None),
        P(DP, None),
        P(DP, None),
        P(),
        P(),
    )
    out_specs = (
        P("slot", None, "hid", DP),
        P("slot", None, "hid", DP),
        P("slot", None, "hid", DP),
        P(DP, ("slot", "hid")),
    )
    return jax.shard_map(
        per_device, mesh=split, in_specs=in_specs, out_specs=out_specs, check_vma=False
    )
```

profile of v0, /device:TPU:2, one launch (start us, length us, event | category | flops | bytes accessed | tf_op | source)
XLA Modules:
  0.0 531.8 jit_solution(10620187443816465604)
XLA Ops:
  7.2 0.0 all-gather.3.cloned.1.call-start
  7.2 1.8 convert_element_type.53
  9.0 0.0 all-gather.3.cloned.1.call-update
  9.1 0.0 reduce-scatter.5.cloned.1.call-start
  9.1 0.7 dynamic_slice.6
  9.8 0.8 fusion.54
  10.7 85.3 %all-gather.3.cloned.1.call-done = bf16[2,3,192,2048]{3,2,1,0:T(8,128)(2,1)} async-done(((bf16[2,3,192,128]{3,2,1,0:T(8,128)(2,1)}), bf16[2,3,192,2048]{3,2,1,0:T(8,128)(2,1)}) %all-gather.3.cloned.1.call-update) | async-done | bytes 4718608 | tf_op jit(solution)/shard_map/all_gather | solution.py:108
  96.0 4.1 fusion.24
  100.1 0.0 copy-start.5
  100.1 3.9 fusion.23
  104.0 1.3 fusion.15
  105.3 1.6 fusion.3
  107.0 0.5 copy-done.6
  107.5 1.1 fusion.14
  108.6 1.2 fusion.13
  109.8 1.5 fusion.26
  111.4 1.5 fusion.25
  112.9 1.3 fusion.10
  114.2 1.6 fusion.6
  115.8 1.1 fusion.9
  116.9 1.4 fusion.8
  118.3 0.2 copy.32
  118.4 0.2 copy.31
  118.6 0.2 copy.30
  118.8 0.2 copy.29
  118.9 0.2 copy.28
  119.1 0.2 copy.27
  119.3 0.6 maximum_maximum_fusion
  119.9 3.4 copy.26
  123.2 0.0 reduce-scatter.5.cloned.1.call-update
  123.2 0.0 reduce-scatter.7.cloned.1.call-start
  123.3 14.0 %reduce-scatter.5.cloned.1.call-done = bf16[8,2,3,192,128]{4,3,2,1,0:T(8,128)(2,1)} async-done(((bf16[16,2,3,192,128]{4,3,2,1,0:T(8,128)(2,1)}), bf16[8,2,3,192,128]{4,3,2,1,0:T(8,128)(2,1)}) %reduce-scatter.5.cloned.1.call-update) | async-done | bytes 2359312 | tf_op jit(solution)/shard_map/reduce_scatter | solution.py:25
  137.3 0.0 reduce-scatter.7.cloned.1.call-update
  137.3 0.0 all-gather.5.cloned.1.call-start
  137.4 105.3 %reduce-scatter.7.cloned.1.call-done = bf16[1,2,3,192,128]{4,3,2,1,0:T(8,128)(2,1)} async-done(((bf16[8,2,3,192,128]{4,3,2,1,0:T(8,128)(2,1)}), bf16[1,2,3,192,128]{4,3,2,1,0:T(8,128)(2,1)}) %reduce-scatter.7.cloned.1.call-update) | async-done | bytes 294928 | tf_op jit(solution)/shard_map/reduce_scatter | solution.py:26
  242.7 2.2 fusion.63
  244.8 0.0 all-gather.5.cloned.1.call-update
  244.9 0.0 reduce-scatter.9.cloned.1.call-start
  244.9 78.6 %all-gather.5.cloned.1.call-done = bf16[2,3,192,2048]{3,2,1,0:T(8,128)(2,1)} async-done(((bf16[2,3,192,128]{3,2,1,0:T(8,128)(2,1)}), bf16[2,3,192,2048]{3,2,1,0:T(8,128)(2,1)}) %all-gather.5.cloned.1.call-update) | async-done | bytes 4718608 | tf_op jit(solution)/shard_map/all_gather | solution.py:162
  323.5 4.1 fusion.22
  327.7 2.7 fusion.21
  330.3 8.6 %fusion.19 = f32[1024,2048]{1,0:T(8,128)} fusion(bf16[1024,2048]{1,0:T(8,128)(2,1)} %param.23, bf16[2,3,192,2048]{3,2,1,0:T(8,128)(2,1)} %all-gather.5.cloned.1.call-done, f32[192,1024]{1,0:T(8,128)S(1)} %fusion.22, f32[1024]{0:T(1024)S(1)} %bitcast.109), kind=kOutput, calls=%fused_computation.29 | convolution fusion | flops 1611988992 | bytes 14946304 | tf_op jit(solution)/shard_map/dot_general | solution.py:69
  338.9 11.1 %convolution_add_fusion = f32[1024,2048]{1,0:T(8,128)} fusion(f32[1024,2048]{1,0:T(8,128)} %fusion.19, bf16[1024,2048]{1,0:T(8,128)(2,1)} %param.23, bf16[2,3,192,2048]{3,2,1,0:T(8,128)(2,1)} %all-gather.5.cloned.1.call-done, f32[192,1024]{1,0:T(8,128)S(1)} %fusion.21, f32[1024]{0:T(1024)S(1)} %bitcast.108), kind=kOutput, calls=%fused_computation.11 | convolution fusion | flops 1614086144 | bytes 23334912 | tf_op jit(solution)/shard_map/dot_general | solution.py:69
  350.0 0.0 reduce-scatter.9.cloned.1.call-update
  350.1 0.6 copy-done.7
  350.7 0.0 copy-done.8
  350.7 0.2 select_reduce_fusion
  350.9 2.1 gather_fusion.4
  353.0 2.2 gather_fusion.2
  355.2 2.2 gather_fusion
  357.3 6.7 %broadcast_select_fusion = (f32[8,3,192,128]{3,2,1,0:T(8,128)}, f32[8,3,192,128]{3,2,1,0:T(8,128)S(1)}, f32[8,3,192,128]{3,2,1,0:T(8,128)}) fusion(f32[8,3,192,128]{3,2,1,0:T(8,128)} %gather_fusion.4, pred[8]{0:T(512)(128)(4,1)S(1)} %get-tuple-element.14, f32[8,3,192,128]{3,2,1,0:T(8,128)} %gather_fusion.2, f32[8,3,192,128]{3,2,1,0:T(8,128)} %gather_fusion), kind=kLoop, calls=%fused_computation.31 | loop fusion | flops 1769472 | bytes 14155784 | tf_op jit(solution)/shard_map/jit(_take)/select_n | solution.py:142
  364.0 4.5 all-to-all-start.2
  368.6 0.0 reduce-scatter.11.cloned.1.call-start
  368.6 85.9 %reduce-scatter.9.cloned.1.call-done = f32[1024,512]{1,0:T(8,128)} async-done(((f32[1024,2048]{1,0:T(8,128)}), f32[1024,512]{1,0:T(8,128)}) %reduce-scatter.9.cloned.1.call-update) | async-done | bytes 2097168 | tf_op jit(solution)/shard_map/reduce_scatter | solution.py:32
  454.5 0.0 reduce-scatter.11.cloned.1.call-update
  454.6 32.7 %all_to_all.15 = f32[4,2,3,192,128]{4,3,2,1,0:T(8,128)} all-to-all(f32[4,2,3,192,128]{4,3,2,1,0:T(8,128)S(1)} %bitcast.98), channel_id=1, replica_groups=mesh['dp_0'=2,'dp_1'=4,'dp_2'=2,'slot'=4,'hid'=4] {'slot'}, dimensions={0} | all-to-all | bytes 4718592 | tf_op jit(solution)/shard_map/all_to_all | solution.py:147
  487.3 3.6 all-to-all-start
  491.0 0.1 compare_and_fusion
  491.1 2.2 gather_fusion.5
  493.3 2.2 gather_fusion.3
  495.6 23.8 %all-to-all-done = f32[4,2,3,192,128]{4,3,2,1,0:T(8,128)S(1)} async-done(((f32[4,2,3,192,128]{4,3,2,1,0:T(8,128)}), f32[4,2,3,192,128]{4,3,2,1,0:T(8,128)S(1)}, u32[]{:S(2)}, u32[]{:S(2)}) %all-to-all-start) | async-done | bytes 2359328 | tf_op jit(solution)/shard_map/all_to_all | solution.py:146
  519.4 1.4 gather_fusion.1
  520.8 2.4 broadcast_select_fusion.3
  523.1 1.8 convert_element_type.66
  (21 shorter events, 0.1 us)
Async XLA Ops:
  7.2 88.8 %all-gather.3.cloned.1.call-start = ((), (), s32[]{:S(2)}) async-start(), calls=%async_computation.7 | async-start | bytes 5013504 | tf_op jit(solution)/shard_map/all_gather | solution.py:108
  9.1 128.2 %reduce-scatter.5.cloned.1.call-start = ((), (), s32[]{:S(2)}) async-start(), calls=%async_computation.8 | async-start | bytes 7077888 | tf_op jit(solution)/shard_map/reduce_scatter | solution.py:25
  96.0 4.1 copy-start.4
  100.1 3.9 copy-start.5
  105.3 2.2 copy-start.6
  123.2 119.5 %copy-start.1 = (f32[2,3,192,128]{3,2,1,0:T(8,128)S(1)}, f32[2,3,192,128]{3,2,1,0:T(8,128)}, u32[]{:S(2)}) copy-start(f32[2,3,192,128]{3,2,1,0:T(8,128)} %param.16) | copy-start | bytes 1769476
  123.2 119.5 %copy-start.2 = (f32[2,3,192,128]{3,2,1,0:T(8,128)S(1)}, f32[2,3,192,128]{3,2,1,0:T(8,128)}, u32[]{:S(2)}) copy-start(f32[2,3,192,128]{3,2,1,0:T(8,128)} %param.17) | copy-start | bytes 1769476
  123.2 119.5 %copy-start.3 = (f32[2,3,192,128]{3,2,1,0:T(8,128)S(1)}, f32[2,3,192,128]{3,2,1,0:T(8,128)}, u32[]{:S(2)}) copy-start(f32[2,3,192,128]{3,2,1,0:T(8,128)} %param.18) | copy-start | bytes 1769476
  123.2 119.4 %reduce-scatter.7.cloned.1.call-start = ((), (), s32[]{:S(2)}) async-start(), calls=%async_computation.9 | async-start | bytes 2654208 | tf_op jit(solution)/shard_map/reduce_scatter | solution.py:26
  137.3 186.2 %all-gather.5.cloned.1.call-start = ((), (), s32[]{:S(2)}) async-start(), calls=%async_computation.10 | async-start | bytes 5013504 | tf_op jit(solution)/shard_map/all_gather | solution.py:162
  244.9 209.7 %reduce-scatter.9.cloned.1.call-start = ((), (), s32[]{:S(2)}) async-start(), calls=%async_computation.11 | async-start | bytes 10485760 | tf_op jit(solution)/shard_map/reduce_scatter | solution.py:32
  323.5 4.1 copy-start
  350.0 0.7 copy-start.7
  350.0 0.7 copy-start.8
  364.0 90.5 %all-to-all-start.2 = ((f32[4,2,3,192,128]{4,3,2,1,0:T(8,128)}), f32[4,2,3,192,128]{4,3,2,1,0:T(8,128)}, u32[]{:S(2)}, u32[]{:S(2)}) async-start(f32[4,2,3,192,128]{4,3,2,1,0:T(8,128)} %bitcast.99), calls=%async_computation.4 | async-start | bytes 4718592 | tf_op jit(solution)/shard_map/all_to_all | solution.py:148
  368.6 154.6 %reduce-scatter.11.cloned.1.call-start = ((), (), s32[]{:S(2)}) async-start(), calls=%async_computation.12 | async-start | bytes 2621440 | tf_op jit(solution)/shard_map/reduce_scatter | solution.py:32
  487.3 32.1 %all-to-all-start = ((f32[4,2,3,192,128]{4,3,2,1,0:T(8,128)}), f32[4,2,3,192,128]{4,3,2,1,0:T(8,128)S(1)}, u32[]{:S(2)}, u32[]{:S(2)}) async-start(f32[4,2,3,192,128]{4,3,2,1,0:T(8,128)} %bitcast.14), calls=%async_computation.2 | async-start | bytes 4718592 | tf_op jit(solution)/shard_map/all_to_all | solution.py:146
Sparse Core Ops, SparseCore 0:
  11.1 84.8 all-gather.2
  123.4 13.8 reduce-scatter.4
  142.0 100.6 reduce-scatter.6
  245.7 77.8 all-gather.4
  350.2 104.3 reduce-scatter.8
  456.9 48.0 reduce-scatter.10
where the time goes:
time: 532 us
  waiting for transfers between devices  393 us (74%)
  matrix products  48.1 us (9%)
  blocking collectives  32.7 us (6%)
  local copies, waits for them, and re-layouts  18.6 us (3%)
  other arithmetic  16.6 us (3%)
  between operations  14.4 us (3%)
  starting transfers between devices  8.42 us (2%)
    reduce_scatter x1, waiting for transfers between devices, summed_rows(): return lax.psum_scatter(pieces, chips, scatter_dimension=0, tiled=True)[0]  105 us
    reduce_scatter x2, waiting for transfers between devices, scatter_axes(): nearer = lax.psum_scatter(x, axes[0], scatter_dimension=dim, tiled=True)  85.9 us
    all_gather x1, waiting for transfers between devices, per_device(): full_weights = lax.all_gather(shard_weights, DP, axis=3, tiled=True)  85.3 us
    all_gather x1, waiting for transfers between devices, per_device(): next_full = lax.all_gather(next_shard, DP, axis=3, tiled=True)  78.6 us
    all_to_all x1, blocking collectives, per_device(): lax.all_to_all(outgoing(new_a), 'slot', split_axis=0, concat_axis=0, tile...  32.7 us
    all_to_all x1, waiting for transfers between devices, per_device(): lax.all_to_all(outgoing(new_master), 'slot', split_axis=0, concat_axis=0,...  23.8 us
    dot_general x8, matrix products, rows_by(): lax.dot_general(left, right, (((1,), (1,)), ((), ())), preferred_element_...  21.1 us
    dot_general x2, matrix products, expert_out(): return jnp.dot(mixed, weights[2], preferred_element_type=jnp.float32)  19.7 us
  transfers between devices with their start and end apart: 8, of which 6 were waited for; matrix products, arithmetic and copies ran while one was open for 4% of the time, Pallas kernels for 0%

commit v1 on v0

--- a/solution.py
+++ b/solution.py
@@ -3,6 +3,7 @@
 from jax import lax
 from jax.sharding import Mesh
 from jax.sharding import PartitionSpec as P
+from jax.lax import axis_index, axis_size, ppermute
 
 DP = ("dp_0", "dp_1", "dp_2")
 learn_rate = 0.001
@@ -142,9 +143,26 @@
         picked = jnp.take(state_block, within, axis=0)
         return picked.reshape((slot_count, local_count) + state_block.shape[1:])
 
+    def screen_unite(z_in, axis_key):
+        all_rows, ready = (axis_size(axis_key), axis_index(axis_key))
+        block_out = list(z_in.shape)
+        next_value = z_in.shape[0] // all_rows
+        block_out[0] = next_value
+        z = block_out[0]
+        block_out[0] = z * all_rows
+        lower = jnp.zeros(block_out, z_in.dtype)
+        for w in tuple(range(all_rows)):
+            x_new = lax.dynamic_slice_in_dim(z_in, (ready ^ w) * next_value, next_value, axis=0)
+            if w:
+                x_new = ppermute(
+                    x_new, axis_name=axis_key, perm=[(ix, ix ^ w) for ix in range(all_rows)]
+                )
+            lower = lax.dynamic_update_slice_in_dim(lower, x_new, (ready ^ w) * z, axis=0)
+        return lower
+
     arrived = (
         lax.all_to_all(outgoing(new_master), "slot", split_axis=0, concat_axis=0, tiled=True),
-        lax.all_to_all(outgoing(new_a), "slot", split_axis=0, concat_axis=0, tiled=True),
+        screen_unite(outgoing(new_a), "slot"),
         lax.all_to_all(outgoing(new_b), "slot", split_axis=0, concat_axis=0, tiled=True),
     )
     moved_states = tuple(

time: 532 us -> 544 us (1.023)
  waiting for transfers between devices: 393 us -> 400 us
  local copies, waits for them, and re-layouts: 18.6 us -> 24.8 us
    ppermute x0 -> x3, waiting for transfers between devices: none -> 45 us  [screen_unite(): ppermute(x_new, axis_name=axis_key, perm=[(ix, ix ^ w) for ix in range(al...]
    all_to_all x1, waiting for transfers between devices: 23.8 us -> 0.01 us  [per_device(): lax.all_to_all(outgoing(new_master), 'slot', split_axis=0, concat_axis=0,...]
    reduce_scatter x2, waiting for transfers between devices: 85.9 us -> 71.9 us  [scatter_axes(): nearer = lax.psum_scatter(x, axes[0], scatter_dimension=dim, tiled=True)]
  transfers between devices with their start and end apart: 8 -> 10, of which waited for: 6 -> 7; matrix products, arithmetic and copies ran while one was open for 4% -> 5% of each run, Pallas kernels for 0% -> 0%
where the time goes in v1:
time: 544 us
  waiting for transfers between devices  400 us (74%)
  matrix products  48.1 us (9%)
  blocking collectives  32.7 us (6%)
  local copies, waits for them, and re-layouts  24.8 us (5%)
  between operations  14.4 us (3%)
  other arithmetic  14.1 us (3%)
  starting transfers between devices  9.66 us (2%)
    reduce_scatter x1, waiting for transfers between devices, summed_rows(): return lax.psum_scatter(pieces, chips, scatter_dimension=0, tiled=True)[0]  105 us
    all_gather x1, waiting for transfers between devices, per_device(): full_weights = lax.all_gather(shard_weights, DP, axis=3, tiled=True)  85.3 us
    all_gather x1, waiting for transfers between devices, per_device(): next_full = lax.all_gather(next_shard, DP, axis=3, tiled=True)  78.6 us
    reduce_scatter x2, waiting for transfers between devices, scatter_axes(): nearer = lax.psum_scatter(x, axes[0], scatter_dimension=dim, tiled=True)  71.9 us
    ppermute x3, waiting for transfers between devices, screen_unite(): ppermute(x_new, axis_name=axis_key, perm=[(ix, ix ^ w) for ix in range(al...  45 us
    all_to_all x1, blocking collectives, per_device(): lax.all_to_all(outgoing(new_b), 'slot', split_axis=0, concat_axis=0, tile...  32.7 us
    dot_general x8, matrix products, rows_by(): lax.dot_general(left, right, (((1,), (1,)), ((), ())), preferred_element_...  21.1 us
    dot_general x2, matrix products, expert_out(): return jnp.dot(mixed, weights[2], preferred_element_type=jnp.float32)  19.7 us
  transfers between devices with their start and end apart: 10, of which 7 were waited for; matrix products, arithmetic and copies ran while one was open for 5% of the time, Pallas kernels for 0%

profile of v1, /device:TPU:2, one launch (start us, length us, event | category | flops | bytes accessed | tf_op | source)
XLA Modules:
  0.0 543.9 jit_solution(7674911993912574130)
XLA Ops:
  7.2 0.0 all-gather.3.cloned.1.call-start
  7.2 1.8 convert_element_type.53
  9.1 0.0 reduce-scatter.5.cloned.1.call-start
  9.1 0.7 dynamic_slice.18
  9.8 0.8 fusion.54
  10.7 85.3 %all-gather.3.cloned.1.call-done = bf16[2,3,192,2048]{3,2,1,0:T(8,128)(2,1)} async-done(((bf16[2,3,192,128]{3,2,1,0:T(8,128)(2,1)}), bf16[2,3,192,2048]{3,2,1,0:T(8,128)(2,1)}) %all-gather.3.cloned.1.call-update) | async-done | bytes 4718608 | tf_op jit(solution)/shard_map/all_gather | solution.py:109
  96.0 4.1 fusion.24
  100.1 3.9 fusion.23
  104.0 1.3 fusion.15
  105.3 1.6 fusion.3
  107.0 0.5 copy-done.6
  107.5 1.1 fusion.14
  108.6 1.2 fusion.13
  109.8 1.5 fusion.26
  111.4 1.5 fusion.25
  112.9 1.3 fusion.10
  114.2 1.6 fusion.6
  115.8 1.1 fusion.9
  116.9 1.4 fusion.8
  118.3 0.2 copy.32
  118.4 0.2 copy.31
  118.6 0.2 copy.30
  118.8 0.2 copy.29
  118.9 0.2 copy.28
  119.1 0.2 copy.27
  119.3 0.6 maximum_maximum_fusion
  119.9 3.4 copy.26
  123.2 0.0 reduce-scatter.7.cloned.1.call-start
  123.3 14.0 %reduce-scatter.5.cloned.1.call-done = bf16[8,2,3,192,128]{4,3,2,1,0:T(8,128)(2,1)} async-done(((bf16[16,2,3,192,128]{4,3,2,1,0:T(8,128)(2,1)}), bf16[8,2,3,192,128]{4,3,2,1,0:T(8,128)(2,1)}) %reduce-scatter.5.cloned.1.call-update) | async-done | bytes 2359312 | tf_op jit(solution)/shard_map/reduce_scatter | solution.py:26
  137.3 0.0 all-gather.5.cloned.1.call-start
  137.4 105.3 %reduce-scatter.7.cloned.1.call-done = bf16[1,2,3,192,128]{4,3,2,1,0:T(8,128)(2,1)} async-done(((bf16[8,2,3,192,128]{4,3,2,1,0:T(8,128)(2,1)}), bf16[1,2,3,192,128]{4,3,2,1,0:T(8,128)(2,1)}) %reduce-scatter.7.cloned.1.call-update) | async-done | bytes 294928 | tf_op jit(solution)/shard_map/reduce_scatter | solution.py:27
  242.7 2.2 fusion.63
  244.9 0.0 reduce-scatter.9.cloned.1.call-start
  244.9 78.6 %all-gather.5.cloned.1.call-done = bf16[2,3,192,2048]{3,2,1,0:T(8,128)(2,1)} async-done(((bf16[2,3,192,128]{3,2,1,0:T(8,128)(2,1)}), bf16[2,3,192,2048]{3,2,1,0:T(8,128)(2,1)}) %all-gather.5.cloned.1.call-update) | async-done | bytes 4718608 | tf_op jit(solution)/shard_map/all_gather | solution.py:180
  323.5 4.1 fusion.22
  327.7 2.7 fusion.21
  330.3 8.6 %fusion.19 = f32[1024,2048]{1,0:T(8,128)} fusion(bf16[1024,2048]{1,0:T(8,128)(2,1)} %param.23, bf16[2,3,192,2048]{3,2,1,0:T(8,128)(2,1)} %all-gather.5.cloned.1.call-done, f32[192,1024]{1,0:T(8,128)S(1)} %fusion.22, f32[1024]{0:T(1024)S(1)} %bitcast.108), kind=kOutput, calls=%fused_computation.29 | convolution fusion | flops 1611988992 | bytes 14946304 | tf_op jit(solution)/shard_map/dot_general | solution.py:70
  338.9 11.1 %convolution_add_fusion = f32[1024,2048]{1,0:T(8,128)} fusion(f32[1024,2048]{1,0:T(8,128)} %fusion.19, bf16[1024,2048]{1,0:T(8,128)(2,1)} %param.23, bf16[2,3,192,2048]{3,2,1,0:T(8,128)(2,1)} %all-gather.5.cloned.1.call-done, f32[192,1024]{1,0:T(8,128)S(1)} %fusion.21, f32[1024]{0:T(1024)S(1)} %bitcast.107), kind=kOutput, calls=%fused_computation.11 | convolution fusion | flops 1614086144 | bytes 23334912 | tf_op jit(solution)/shard_map/dot_general | solution.py:70
  350.1 0.0 reduce-scatter.11.cloned.1.call-start
  350.1 0.6 copy-done.7
  350.7 0.2 select_reduce_fusion
  350.9 2.1 gather_fusion.4
  353.0 2.2 gather_fusion.2
  355.2 2.2 gather_fusion
  357.4 71.9 %reduce-scatter.9.cloned.1.call-done = f32[1024,512]{1,0:T(8,128)} async-done(((f32[1024,2048]{1,0:T(8,128)}), f32[1024,512]{1,0:T(8,128)}) %reduce-scatter.9.cloned.1.call-update) | async-done | bytes 2097168 | tf_op jit(solution)/shard_map/reduce_scatter | solution.py:33
  429.3 5.3 broadcast_select_fusion
  434.6 32.7 %all_to_all.10 = f32[4,2,3,192,128]{4,3,2,1,0:T(8,128)} all-to-all(f32[4,2,3,192,128]{4,3,2,1,0:T(8,128)S(1)} %bitcast.99), channel_id=1, replica_groups=mesh['dp_0'=2,'dp_1'=4,'dp_2'=2,'slot'=4,'hid'=4] {'slot'}, dimensions={0} | all-to-all | bytes 4718592 | tf_op jit(solution)/shard_map/all_to_all | solution.py:166
  467.3 4.7 all-to-all-start
  472.1 1.7 broadcast_in_dim.64
  473.8 1.0 constant_dynamic-slice_fusion
  474.8 1.7 collective-permute-start
  476.6 2.7 collective-permute-start.1
  479.2 0.3 collective-permute-start.2
  479.5 0.1 compare_and_fusion
  479.6 34.0 %collective-permute-done = f32[1,2,3,192,128]{4,3,2,1,0:T(8,128)S(1)} collective-permute-done((f32[1,2,3,192,128]{4,3,2,1,0:T(8,128)S(1)}, f32[1,2,3,192,128]{4,3,2,1,0:T(8,128)S(1)}, u32[]{:S(2)}, u32[]{:S(2)}) %collective-permute-start) | collective-permute-done | bytes 589856 | tf_op jit(solution)/shard_map/ppermute | solution.py:157
  513.6 0.9 constant_dynamic-update-slice_fusion.1
  514.4 11.0 %collective-permute-done.1 = f32[1,2,3,192,128]{4,3,2,1,0:T(8,128)S(1)} collective-permute-done((f32[1,2,3,192,128]{4,3,2,1,0:T(8,128)S(1)}, f32[1,2,3,192,128]{4,3,2,1,0:T(8,128)S(1)}, u32[]{:S(2)}, u32[]{:S(2)}) %collective-permute-start.1) | collective-permute-done | bytes 589856 | tf_op jit(solution)/shard_map/ppermute | solution.py:157
  525.4 0.9 constant_dynamic-update-slice_fusion
  526.3 0.9 constant_dynamic-update-slice_fusion.2
  527.2 2.2 gather_fusion.3
  529.4 2.2 gather_fusion.5
  531.7 2.2 gather_fusion.1
  534.0 1.3 broadcast_select_fusion.3
  535.3 1.8 convert_element_type.66
  (30 shorter events, 0.2 us)
Async XLA Ops:
  7.2 88.8 %all-gather.3.cloned.1.call-start = ((), (), s32[]{:S(2)}) async-start(), calls=%async_computation.6 | async-start | bytes 5013504 | tf_op jit(solution)/shard_map/all_gather | solution.py:109
  9.1 128.2 %reduce-scatter.5.cloned.1.call-start = ((), (), s32[]{:S(2)}) async-start(), calls=%async_computation.7 | async-start | bytes 7077888 | tf_op jit(solution)/shard_map/reduce_scatter | solution.py:26
  96.0 4.1 copy-start.4
  100.1 3.9 copy-start.5
  105.3 2.2 copy-start.6
  123.2 119.5 %copy-start.1 = (f32[2,3,192,128]{3,2,1,0:T(8,128)S(1)}, f32[2,3,192,128]{3,2,1,0:T(8,128)}, u32[]{:S(2)}) copy-start(f32[2,3,192,128]{3,2,1,0:T(8,128)} %param.16) | copy-start | bytes 1769476
  123.2 119.5 %copy-start.2 = (f32[2,3,192,128]{3,2,1,0:T(8,128)S(1)}, f32[2,3,192,128]{3,2,1,0:T(8,128)}, u32[]{:S(2)}) copy-start(f32[2,3,192,128]{3,2,1,0:T(8,128)} %param.17) | copy-start | bytes 1769476
  123.2 119.5 %copy-start.3 = (f32[2,3,192,128]{3,2,1,0:T(8,128)S(1)}, f32[2,3,192,128]{3,2,1,0:T(8,128)}, u32[]{:S(2)}) copy-start(f32[2,3,192,128]{3,2,1,0:T(8,128)} %param.18) | copy-start | bytes 1769476
  123.2 119.4 %reduce-scatter.7.cloned.1.call-start = ((), (), s32[]{:S(2)}) async-start(), calls=%async_computation.8 | async-start | bytes 2654208 | tf_op jit(solution)/shard_map/reduce_scatter | solution.py:27
  137.3 186.2 %all-gather.5.cloned.1.call-start = ((), (), s32[]{:S(2)}) async-start(), calls=%async_computation.9 | async-start | bytes 5013504 | tf_op jit(solution)/shard_map/all_gather | solution.py:180
  244.9 184.4 %reduce-scatter.9.cloned.1.call-start = ((), (), s32[]{:S(2)}) async-start(), calls=%async_computation.10 | async-start | bytes 10485760 | tf_op jit(solution)/shard_map/reduce_scatter | solution.py:33
  323.5 4.1 copy-start
  350.1 0.7 copy-start.7
  350.1 0.7 copy-start.8
  350.1 185.2 %reduce-scatter.11.cloned.1.call-start = ((), (), s32[]{:S(2)}) async-start(), calls=%async_computation.11 | async-start | bytes 2621440 | tf_op jit(solution)/shard_map/reduce_scatter | solution.py:33
  467.3 64.4 %all-to-all-start = ((f32[4,2,3,192,128]{4,3,2,1,0:T(8,128)}), f32[4,2,3,192,128]{4,3,2,1,0:T(8,128)}, u32[]{:S(2)}, u32[]{:S(2)}) async-start(f32[4,2,3,192,128]{4,3,2,1,0:T(8,128)} %bitcast.14), calls=%async_computation.2 | async-start | bytes 4718592 | tf_op jit(solution)/shard_map/all_to_all | solution.py:164
  474.8 38.8 %collective-permute-start = (f32[1,2,3,192,128]{4,3,2,1,0:T(8,128)S(1)}, f32[1,2,3,192,128]{4,3,2,1,0:T(8,128)S(1)}, u32[]{:S(2)}, u32[]{:S(2)}) collective-permute-start(f32[1,2,3,192,128]{4,3,2,1,0:T(8,128)S(1)} %get-tuple-element.18), channel_id=1, source_target_pairs={{0,4},{4,0},{8,12},{12,8},{1,5},{5,1},{9,13},{13,9},{2,6},{6,2},{1... | collective-permute-start | bytes 1769480 | tf_op jit(solution)/shard_map/ppermute | solution.py:157
  476.6 48.9 %collective-permute-start.1 = (f32[1,2,3,192,128]{4,3,2,1,0:T(8,128)S(1)}, f32[1,2,3,192,128]{4,3,2,1,0:T(8,128)S(1)}, u32[]{:S(2)}, u32[]{:S(2)}) collective-permute-start(f32[1,2,3,192,128]{4,3,2,1,0:T(8,128)S(1)} %get-tuple-element.17), channel_id=1, source_target_pairs={{0,8},{4,12},{8,0},{12,4},{1,9},{5,13},{9,1},{13,5},{2,10},{6,14},... | collective-permute-start | bytes 1769480 | tf_op jit(solution)/shard_map/ppermute | solution.py:157
  479.2 47.1 %collective-permute-start.2 = (f32[1,2,3,192,128]{4,3,2,1,0:T(8,128)S(1)}, f32[1,2,3,192,128]{4,3,2,1,0:T(8,128)S(1)}, u32[]{:S(2)}, u32[]{:S(2)}) collective-permute-start(f32[1,2,3,192,128]{4,3,2,1,0:T(8,128)S(1)} %get-tuple-element.16), channel_id=1, source_target_pairs={{0,12},{4,8},{8,4},{12,0},{1,13},{5,9},{9,5},{13,1},{2,14},{6,10},... | collective-permute-start | bytes 1769480 | tf_op jit(solution)/shard_map/ppermute | solution.py:157
Sparse Core Ops, SparseCore 0:
  11.1 84.8 all-gather.2
  123.4 13.8 reduce-scatter.4
  142.0 100.6 reduce-scatter.6
  245.7 77.8 all-gather.4
  350.2 79.0 reduce-scatter.8
  431.7 48.8 reduce-scatter.10
